TPU v7x, 32 devices: a whole 2x2x4 slice. The times are simulated.
32 devices in a mesh: seq: 8 (over z, y), dp: 4 (over x, core).
Axes of the slice: x: 2, y: 2, z: 4, core: 2. Of those that a mesh axis runs over, the one named last changes fastest.
Arguments:
- queries: bfloat16 [4, 3072, 2048], P('dp', 'seq'), may hold values from -0.59765625 to 0.59765625
- keys: bfloat16 [4, 3072, 2048], P('dp', 'seq'), may hold values from -0.59765625 to 0.59765625
- values: bfloat16 [4, 3072, 2048], P('dp', 'seq'), may hold values from -6 to 6
- output_gradient: bfloat16 [4, 3072, 2048], P('dp', 'seq'), may hold values from -0.59765625 to 0.59765625
- document_lengths: int32 [4, 8], P('dp'), may hold values from 1 to 768, 3072 in all within a row
- cutoff_rows: int32 [4, 3072], P('dp', 'seq'), may hold values 0 or 1
- head_decay_rate: float32 [16], replicated, may hold values from 1.6276042e-05 to 0.04, as said below
Outputs:
- query_grad: bfloat16 [4, 3072, 2048], P('dp', 'seq')
- key_grad: bfloat16 [4, 3072, 2048], P('dp', 'seq')
- value_grad: bfloat16 [4, 3072, 2048], P('dp', 'seq')
- rate_grad: float32 [16], replicated
Inputs may be any that keep to these rules, and one draw needn't show every extreme that they name: `head_decay_rate`: a positive rate for each head.
All inputs are finite; a program needn't handle non-finite values. No bound on the sum of `cutoff_rows` on one device may be relied on, other than what follows from the above.
Results may differ from a plain program's by a relative error of at most 0.0034.
Values sent between devices are 32-bit elements; how exact they have to be, the bound alone decides.
A program may use at most 192 MiB of HBM per device.

v0:
```python
import math

import jax
import jax.numpy as jnp
from jax import lax
from jax.sharding import PartitionSpec as P

HEADS = 16
HEAD_DIM = 128


cutoff_logarithm = math.log(0.7)
state_mode = lax.Precision.HIGH


def carried_in(part, axis, combine, identity, reverse):
    count = lax.axis_size(axis)
    place = lax.axis_index(axis)
    ahead = count - 1 - place if reverse else place
    gathered = jax.tree.map(lambda a: lax.all_gather(a, axis), part)
    state = jax.tree.map(lambda a, e: jnp.zeros_like(a) + jnp.asarray(e, a.dtype), part, identity)

    def one(step, state):
        source = count - 1 - step if reverse else step
        return combine(
            state, jax.tree.map(lambda a: lax.dynamic_index_in_dim(a, source, 0, False), gathered)
        )

    return lax.fori_loop(0, ahead, one, state)


def block_mask_list(head_decay_rate, cutoff_list, row_position, start_list):
    is_start = jnp.any(row_position[:, None] == start_list[None, :], axis=1)
    seg_local = jnp.cumsum(is_start.astype(jnp.int32))
    begin = jnp.max(
        jnp.where(start_list[None, :] <= row_position[:, None], start_list[None, :], 0), axis=1
    )
    position = (row_position - begin).astype(jnp.float32)
    logarithm_step = (
        cutoff_list.astype(jnp.float32)[:, None] * cutoff_logarithm - head_decay_rate[None, :]
    )
    cum_log = jnp.cumsum(logarithm_step, axis=0)
    carry_in = jnp.where((seg_local == 0)[:, None], jnp.exp(cum_log), 0.0)
    carry_out = jnp.where(
        (seg_local == seg_local[-1])[:, None], jnp.exp(cum_log[-1][None, :] - cum_log), 0.0
    )
    decay_all = jnp.where(seg_local[-1] == 0, jnp.exp(cum_log[-1]), 0.0)
    return (cum_log, seg_local, position, carry_in, carry_out, decay_all)


def weights_of(cum_log, seg_local):
    count = seg_local.shape[0]
    index = jnp.arange(count, dtype=jnp.int32)
    allowed = (seg_local[:, None] == seg_local[None, :]) & (index[:, None] >= index[None, :])
    spread = cum_log.T[:, :, None] - cum_log.T[:, None, :]
    return jnp.where(allowed[None], jnp.exp(jnp.where(allowed[None], spread, 0.0)), 0.0)


def forward_combine(earlier, later):
    return (earlier[0] * later[0], later[0][:, None, None] * earlier[1] + later[1])


def backward_combine(earlier, later):
    return (later[0] * earlier[0], later[1] + later[0][:, None, None] * earlier[1])


def on_device(
    queries, keys, values, output_gradient, document_lengths, cutoff_rows, head_decay_rate
):
    row_count = queries.shape[1]
    query_block = queries.reshape(row_count, HEADS, HEAD_DIM)
    key_block = keys.reshape(row_count, HEADS, HEAD_DIM)
    value_block = values.reshape(row_count, HEADS, HEAD_DIM)
    gradient_block = output_gradient.reshape(row_count, HEADS, HEAD_DIM)
    block_piece = lax.axis_index("seq")
    row_position = block_piece * row_count + jnp.arange(row_count, dtype=jnp.int32)
    length_list = document_lengths[0]
    start_list = jnp.cumsum(length_list) - length_list
    cum_log, seg_local, position, carry_in, carry_out, decay_all = block_mask_list(
        head_decay_rate, cutoff_rows[0], row_position, start_list
    )
    key_f = key_block.astype(jnp.float32)
    value_f = value_block.astype(jnp.float32)
    grad_f = gradient_block.astype(jnp.float32)
    query_f = query_block.astype(jnp.float32)
    state_local = jnp.einsum(
        "the,thf->hef", carry_out[:, :, None] * key_f, value_f, precision=state_mode
    )
    back_local = jnp.einsum(
        "she,shf->hef", carry_in[:, :, None] * query_f, grad_f, precision=state_mode
    )
    identity = (jnp.ones_like(decay_all), jnp.zeros_like(state_local))
    state_input = carried_in((decay_all, state_local), "seq", forward_combine, identity, False)[1]
    backward_input = carried_in((decay_all, back_local), "seq", backward_combine, identity, True)[1]
    weight = weights_of(cum_log, seg_local)
    scores = jnp.einsum("she,the->hst", query_block, key_block, preferred_element_type=jnp.float32)
    grad_scores = jnp.einsum(
        "shf,thf->hst", gradient_block, value_block, preferred_element_type=jnp.float32
    )
    attn_prob = (weight * scores).astype(jnp.bfloat16)
    grad_prob = (weight * grad_scores).astype(jnp.bfloat16)
    value_full = jnp.einsum(
        "hst,shf->thf", attn_prob, gradient_block, preferred_element_type=jnp.float32
    )
    value_full = value_full + carry_out[:, :, None] * jnp.einsum(
        "the,hef->thf", key_f, backward_input, precision=state_mode
    )
    query_full = jnp.einsum(
        "hst,the->she", grad_prob, key_block, preferred_element_type=jnp.float32
    )
    query_full = query_full + carry_in[:, :, None] * jnp.einsum(
        "shf,hef->she", grad_f, state_input, precision=state_mode
    )
    key_full = jnp.einsum(
        "hst,she->the", grad_prob, query_block, preferred_element_type=jnp.float32
    )
    key_full = key_full + carry_out[:, :, None] * jnp.einsum(
        "thf,hef->the", value_f, backward_input, precision=state_mode
    )
    inner_step = jnp.sum(key_f * key_full, axis=2) - jnp.sum(query_f * query_full, axis=2)
    rate_part = jnp.sum(position[:, None] * inner_step, axis=0)
    rate_total = lax.psum(rate_part, ("seq", "dp"))
    token_total = row_count * lax.axis_size("seq") * lax.axis_size("dp")
    rate_grad = head_decay_rate * rate_total / math.sqrt(token_total)
    out_shape = (1, row_count, HEADS * HEAD_DIM)
    return (
        query_full.astype(jnp.bfloat16).reshape(out_shape),
        key_full.astype(jnp.bfloat16).reshape(out_shape),
        value_full.astype(jnp.bfloat16).reshape(out_shape),
        rate_grad,
    )


def solution(mesh):
    in_specs = (
        P("dp", "seq", None),
        P("dp", "seq", None),
        P("dp", "seq", None),
        P("dp", "seq", None),
        P("dp", None),
        P("dp", "seq"),
        P(),
    )
    out_specs = (P("dp", "seq", None), P("dp", "seq", None), P("dp", "seq", None), P())
    return jax.shard_map(
        on_device, mesh=mesh, in_specs=in_specs, out_specs=out_specs, check_vma=False
    )
```

profile of v0, /device:TPU:0, one launch (start us, length us, event | category | flops | bytes accessed | tf_op | source)
XLA Modules:
  0.0 359.1 jit_solution(17333304363700179189)
XLA Ops:
  7.2 0.0 all-gather.8.cloned.1.call-start
  7.2 0.8 reduce-window_clone.1
  8.0 0.7 subtract_bitcast_fusion
  8.7 0.1 compare_reduce_fusion
  8.8 0.3 reduce-window.16
  9.1 0.1 slice.21
  9.2 0.1 slice_reduce_fusion.2
  9.3 0.1 broadcast_compare_fusion.1
  9.4 0.6 slice.25
  10.7 0.7 broadcast_compare_fusion
  11.3 0.7 multiply_reduce_fusion.1
  12.0 0.7 broadcast_subtract_fusion
  12.7 0.9 reduce-window.24
  13.6 0.2 slice_reduce_fusion
  13.8 0.1 copy_bitcast_fusion
  13.9 1.9 copy.84
  15.8 0.0 copy-start
  15.8 2.4 copy.99
  18.2 0.0 copy-start.2
  18.2 0.2 slice_reduce_fusion.1
  18.4 0.1 exponential_select_fusion.2
  18.5 2.4 fusion.9
  20.9 0.0 copy-done
  20.9 0.0 all-gather.8.cloned.1.call-update
  20.9 0.0 all-gather.6.cloned.1.call-start
  21.0 1.9 copy.81
  22.9 1.8 copy.101
  24.7 0.0 copy-start.3
  24.7 1.1 copy-done.3
  25.8 2.4 fusion.7
  28.3 0.0 all-gather.6.cloned.1.call-update
  28.3 22.4 %all-gather.2 = f32[8,1,16]{2,1,0:T(1,128)S(1)} all-gather(f32[1,1,16]{2,1,0:T(1,128)S(1)} %bitcast.115), channel_id=1, replica_groups=mesh['seq'=8,'dp'=4] {'seq'}, dimensions={0}, use_global_device_ids=true | all-gather | bytes 576 | tf_op jit(solution)/shard_map/all_gather | solution.py:20
  50.7 0.1 select_reduce_fusion
  50.8 0.1 fusion.21
  50.9 0.0 copy-done.2
  50.9 6.8 %multiply_convert_fusion.1 = bf16[16,384,384]{2,1,0:T(8,128)(2,1)} fusion(f32[16,384]{1,0:T(8,128)S(1)} %get-tuple-element.184, pred[384,384]{1,0:T(8,128)(4,1)S(1)} %fusion.21, bf16[384,16,128]{0,2,1:T(8,128)(2,1)S(1)} %bitcast.99, bf16[384,16,128]{2,1,0:T(8,128)(2,1)} %bitcast.103), kind=kOutput, calls=%fused_computation.5 | convolution fusion | flops 615776256 | bytes 8036352 | tf_op jit(solution)/shard_map/shf,thf->hst/dot_general | solution.py:97
  57.8 90.9 %all-gather.8.cloned.1.call-done = f32[128,128,128]{2,1,0:T(8,128)} async-done(((f32[16,128,128]{2,1,0:T(8,128)}), f32[128,128,128]{2,1,0:T(8,128)}) %all-gather.8.cloned.1.call-update) | async-done | bytes 8388624 | tf_op jit(solution)/shard_map/all_gather | solution.py:20
  148.7 0.1 broadcast_in_dim.82.clone.1
  148.8 10.7 %while.27 = (s32[]{:T(128)}, f32[16,128,128]{2,1,0:T(8,128)S(1)}, s32[]{:T(128)}, f32[8,16,128,128]{3,2,1,0:T(8,128)}, f32[8,16]{1,0:T(8,128)S(1)}, /*index=5*/s32[]{:T(128)}, s32[]{:T(128)}, s32[]{:T(128)}, s32[]{:T(128)}) while((s32[]{:T(128)}, f32[16,128,128]{2,1,0:T(8,128)S(1)}, s32[]{:T(128)}, f32[8,16,128,128]{3,2,1,0:T(8,128)}, ...), condition=%wide.region_9.10_spmd, body=%wide.region_8.9_spmd.sunk | while | flops 524294 | bytes 3146075 | solution.py:29
  148.9 1.4 bitcast_add_fusion.5
  150.4 1.4 bitcast_add_fusion.5
  151.8 1.4 bitcast_add_fusion.5
  153.3 1.5 bitcast_add_fusion.5
  154.8 1.5 bitcast_add_fusion.5
  156.4 1.6 bitcast_add_fusion.5
  158.0 1.5 bitcast_add_fusion.5
  159.6 4.6 %fusion.17 = f32[16,128,384]{2,1,0:T(8,128)} fusion(f32[16,128,128]{2,1,0:T(8,128)S(1)} %get-tuple-element.133, bf16[384,16,128]{2,1,0:T(8,128)(2,1)} %bitcast.104), kind=kOutput, calls=%fused_computation.30 | convolution fusion | flops 603979776 | bytes 5767168 | tf_op jit(solution)/shard_map/thf,hef->the/dot_general | solution.py:117
  164.2 2.8 fusion.25
  167.0 107.0 %all-gather.6.cloned.1.call-done = f32[128,128,128]{2,1,0:T(8,128)} async-done(((f32[16,128,128]{2,1,0:T(8,128)}), f32[128,128,128]{2,1,0:T(8,128)}) %all-gather.6.cloned.1.call-update) | async-done | bytes 8388624 | tf_op jit(solution)/shard_map/all_gather | solution.py:20
  274.0 0.1 broadcast_in_dim.82.clone
  274.1 0.2 while.26
  274.3 4.0 %fusion.24 = f32[16,128,384]{2,1,0:T(8,128)} fusion(f32[16,128,128]{2,1,0:T(8,128)S(1)} %get-tuple-element.132, bf16[384,16,128]{0,2,1:T(8,128)(2,1)} %bitcast.100), kind=kOutput, calls=%fused_computation.59 | convolution fusion | flops 603979776 | bytes 5767168 | tf_op jit(solution)/shard_map/shf,hef->she/dot_general | solution.py:111
  278.3 8.2 %fusion.12 = bf16[384,16,128]{0,2,1:T(8,128)(2,1)} fusion(f32[16,128,384]{2,1,0:T(8,128)} %fusion.25, bf16[384,16,128]{0,2,1:T(8,128)(2,1)} %bitcast.101, f32[16,384]{1,0:T(8,128)S(1)} %get-tuple-element.184, pred[384,384]{1,0:T(8,128)(4,1)S(1)} %fusion.21, bf16[384,16,128]{0,2,1:T(8,128)(2,1)} %bitcast.95, bf16[384,16,128]{0,2,1:T(8,128)(2,1)S(1)} %bitcast.91, ...), kind=kOutput, calls=%fused_computation.23 | convolution fusion | flops 1222115328 | bytes 9633792 | tf_op jit(solution)/shard_map/hst,shf->thf/dot_general | solution.py:102
  286.6 2.7 copy.94
  289.3 0.0 copy-done.1
  289.3 5.9 %fusion.8 = (f32[384,16]{0,1:T(8,128)S(1)}, bf16[384,16,128]{0,2,1:T(8,128)(2,1)}) fusion(bf16[384,16,128]{0,2,1:T(8,128)(2,1)S(1)} %bitcast.92, f32[16,128,384]{2,1,0:T(8,128)} %fusion.17, f32[384,16]{0,1:T(8,128)S(1)} %get-tuple-element.183, bf16[384,16,128]{0,2,1:T(8,128)(2,1)S(1)} %bitcast.96, bf16[16,384,384]{2,1,0:T(8,128)(2,1)} %multiply_convert_fusion.1), kind=kOutput, calls=%fused_computation.18 | convolution fusion | flops 608692224 | bytes 12632064 | tf_op jit(solution)/shard_map/hst,she->the/dot_general | solution.py:114
  295.1 0.0 copy-done.4
  295.1 5.1 %fusion.10 = (f32[384,16]{0,1:T(8,128)S(1)}, bf16[384,16,128]{0,2,1:T(8,128)(2,1)}) fusion(bf16[384,16,128]{0,2,1:T(8,128)(2,1)S(1)} %bitcast.97, f32[16,128,384]{2,1,0:T(8,128)S(1)} %copy-done.4, f32[384,16]{0,1:T(8,128)S(1)} %get-tuple-element.182, bf16[16,384,384]{2,1,0:T(8,128)(2,1)} %multiply_convert_fusion.1, bf16[384,16,128]{0,2,1:T(8,128)(2,1)S(1)} %bitcast.93), kind=kOutput, calls=%fused_computation.20 | convolution fusion | flops 608692224 | bytes 12632064 | tf_op jit(solution)/shard_map/hst,the->she/dot_general | solution.py:108
  300.2 0.1 multiply_reduce_fusion
  300.3 2.7 copy.92
  303.0 47.1 %psum.7 = f32[16]{0:T(128)S(1)} all-reduce(f32[16]{0:T(128)S(1)} %multiply_reduce_fusion), channel_id=1, replica_groups=mesh['seq'=8,'dp'=4] {'seq','dp'}, use_global_device_ids=true, to_apply=%region_14.15 | all-reduce | flops 16 | bytes 128 | tf_op jit(solution)/shard_map/psum | solution.py:122
  350.1 0.0 copy-done.6
  350.1 0.5 multiply_multiply_fusion
  350.6 1.6 copy.93
  (17 shorter events, 0.2 us)
Async XLA Ops:
  7.2 141.6 %all-gather.8.cloned.1.call-start = ((), (), s32[]{:S(2)}) async-start(), calls=%async_computation.1 | async-start | bytes 9437184 | tf_op jit(solution)/shard_map/all_gather | solution.py:20
  15.8 5.2 %copy-start = (bf16[1,384,2048]{1,2,0:T(8,128)(2,1)}, bf16[1,384,2048]{1,2,0:T(8,128)(2,1)S(1)}, u32[]{:S(2)}) copy-start(bf16[1,384,2048]{1,2,0:T(8,128)(2,1)S(1)} %copy.84) | copy-start | bytes 4718596
  18.2 32.7 %copy-start.2 = (bf16[1,384,2048]{1,2,0:T(8,128)(2,1)}, bf16[1,384,2048]{1,2,0:T(8,128)(2,1)S(1)}, u32[]{:S(2)}) copy-start(bf16[1,384,2048]{1,2,0:T(8,128)(2,1)S(1)} %copy.99) | copy-start | bytes 4718596
  20.9 253.1 %all-gather.6.cloned.1.call-start = ((), (), s32[]{:S(2)}) async-start(), calls=%async_computation | async-start | bytes 9437184 | tf_op jit(solution)/shard_map/all_gather | solution.py:20
  24.7 1.1 copy-start.3
  286.6 2.7 copy-start.1
  289.3 5.9 %copy-start.4 = (f32[16,128,384]{2,1,0:T(8,128)S(1)}, f32[16,128,384]{2,1,0:T(8,128)}, u32[]{:S(2)}) copy-start(f32[16,128,384]{2,1,0:T(8,128)} %fusion.24) | copy-start | bytes 9437188
  300.2 49.9 %copy-start.6 = (f32[16]{0:T(128)S(1)}, f32[16]{0:T(128)}, u32[]{:S(2)}) copy-start(f32[16]{0:T(128)} %param.17) | copy-start | bytes 196
  300.2 50.4 %copy-start.5 = (bf16[384,16,128]{0,2,1:T(8,128)(2,1)S(1)}, bf16[384,16,128]{0,2,1:T(8,128)(2,1)}, u32[]{:S(2)}) copy-start(bf16[384,16,128]{0,2,1:T(8,128)(2,1)} %get-tuple-element.181) | copy-start | bytes 4718596
Sparse Core Ops, SparseCore 0:
  21.1 127.6 all-gather.7
  150.8 123.1 all-gather.5
where the time goes:
time: 360 us; the launch traced here: 359 us
  waiting for transfers between devices  198 us (55%)
  blocking collectives  69.5 us (19%)
  matrix products  42.3 us (12%)
  local copies, waits for them, and re-layouts  17.4 us (5%)
  other arithmetic  16.6 us (5%)
  between operations  14.8 us (4%)
    all_gather x2, waiting for transfers between devices, carried_in(): gathered = jax.tree.map(lambda a: lax.all_gather(a, axis), part)  198 us
    psum x1, blocking collectives, on_device(): rate_total = lax.psum(rate_part, ('seq', 'dp'))  47.1 us
    all_gather x1, blocking collectives, carried_in(): gathered = jax.tree.map(lambda a: lax.all_gather(a, axis), part)  22.4 us
    unnamed x20, local copies, waits for them, and re-layouts  13.7 us
    add x7, other arithmetic, backward_combine(): later[1] + later[0][:, None, None] * earlier[1]  10.4 us
    dot_general x1, matrix products, on_device(): jnp.einsum('hst,shf->thf', attn_prob, gradient_block, preferred_element_t...  8.23 us
  transfers between devices with their start and end apart: 2, of which 2 were waited for; matrix products, arithmetic and copies ran while one was open for 9% of the time, Pallas kernels for 0%

commit v1 on v0

--- a/solution.py
+++ b/solution.py
@@ -1,8 +1,11 @@
+import functools
 import math
 
 import jax
 import jax.numpy as jnp
 from jax import lax
+from jax.experimental import pallas as pl
+from jax.experimental.pallas import tpu as pltpu
 from jax.sharding import PartitionSpec as P
 
 HEADS = 16
@@ -131,6 +134,455 @@
     )
 
 
+MESH_ID = pl.DeviceIdType.MESH
+CHUNK_HEADS = 2
+CHUNKS = HEADS // CHUNK_HEADS
+MASKED = -1e30
+
+
+def dot(a, b, contract):
+    return lax.dot_general(
+        a, b, ((contract[:1], contract[1:]), ((), ())), preferred_element_type=jnp.float32
+    )
+
+
+def halves(array):
+    high = array.astype(jnp.bfloat16)
+    return high, (array - high.astype(jnp.float32)).astype(jnp.bfloat16)
+
+
+def near_kernel(
+    lengths,
+    rates,
+    cutoffs,
+    queries,
+    keys,
+    values,
+    gradients,
+    query_out,
+    key_out,
+    value_out,
+    rate_out,
+    spread,
+    distance,
+    log_in,
+    log_out,
+    place,
+    decays,
+    near_decays,
+    states,
+    from_pair,
+    from_line,
+    relayed,
+    query_sum,
+    key_sum,
+    value_sum,
+    rate_rows,
+    rate_dp,
+    rate_seq,
+    pair_send,
+    pair_recv,
+    line_send,
+    line_recv,
+    relay_send,
+    relay_recv,
+    decay_send,
+    decay_recv,
+    dp_send,
+    dp_recv,
+    seq_send,
+    seq_recv,
+):
+    n_seq, n_dp = lax.axis_size("seq"), lax.axis_size("dp")
+    block, part = lax.axis_index("seq"), lax.axis_index("dp")
+    rows = queries.shape[0]
+    side = lax.rem(block, 2)
+    pair = block + 1 - 2 * side
+    is_first, is_last = block < 2, block >= n_seq - 2
+    has_relay = jnp.where(side == 1, block, n_seq - 1 - block) >= 2
+    gets_relay = jnp.where(side == 0, block, n_seq - 1 - block) >= 2
+
+    barrier = pltpu.get_barrier_semaphore()
+    for other in range(1, n_seq):
+        pl.semaphore_signal(
+            barrier,
+            inc=1,
+            device_id={"seq": lax.rem(block + other, n_seq)},
+            device_id_type=MESH_ID,
+        )
+    for other in range(1, n_dp):
+        pl.semaphore_signal(
+            barrier, inc=1, device_id={"dp": lax.rem(part + other, n_dp)}, device_id_type=MESH_ID
+        )
+
+    first = block * rows
+    starts, total = [], jnp.int32(0)
+    for j in range(lengths.shape[1]):
+        starts.append(total)
+        total = total + lengths[0, j]
+
+    def segment(local):
+        count = jnp.zeros(local.shape, jnp.int32)
+        for start in starts:
+            count = count + jnp.where((start >= first) & (local + first >= start), 1, 0)
+        return count
+
+    row_of = lax.broadcasted_iota(jnp.int32, (rows, rows), 0)
+    column_of = lax.broadcasted_iota(jnp.int32, (rows, rows), 1)
+    cut_row = cutoffs[...].astype(jnp.float32)
+    cut_all = jnp.broadcast_to(cut_row, (rows, rows))
+    count_column = jnp.sum(jnp.where(column_of <= row_of, cut_all, 0.0), axis=1, keepdims=True)
+    cut_column = jnp.sum(jnp.where(column_of == row_of, cut_all, 0.0), axis=1, keepdims=True)
+    count_row = jnp.sum(jnp.where(row_of <= column_of, cut_column, 0.0), axis=0, keepdims=True)
+    count_last = jnp.sum(cut_row, axis=1, keepdims=True)
+    allowed = (segment(row_of) == segment(column_of)) & (row_of >= column_of)
+    spread[...] = jnp.where(allowed, (count_column - count_row) * cutoff_logarithm, MASKED)
+    distance[...] = (row_of - column_of).astype(jnp.float32)
+    local = lax.broadcasted_iota(jnp.int32, (rows, HEAD_DIM), 0)
+    last = jnp.full((rows, HEAD_DIM), rows - 1, jnp.int32)
+    piece = segment(local)
+    piece_last = segment(last)
+    log_in[...] = jnp.where(piece == 0, count_column * cutoff_logarithm, MASKED)
+    log_out[...] = jnp.where(
+        piece == piece_last, (count_last - count_column) * cutoff_logarithm, MASKED
+    )
+    begin = jnp.zeros((rows, HEAD_DIM), jnp.int32)
+    for start in starts:
+        begin = jnp.maximum(begin, jnp.where(local + first >= start, start, 0))
+    place[...] = (local + first - begin).astype(jnp.float32)
+    log_all = jnp.where(piece_last[:1] == 0, count_last * cutoff_logarithm, MASKED)
+    for h in range(HEADS):
+        decays[h : h + 1, :] = jnp.exp(log_all - rates[h] * float(rows))
+
+    @pl.when(is_first)
+    def _():
+        from_line[0] = jnp.zeros(from_line.shape[1:], jnp.float32)
+
+    @pl.when(is_last)
+    def _():
+        from_line[1] = jnp.zeros(from_line.shape[1:], jnp.float32)
+
+    @pl.when(block == 0)
+    def _():
+        near_decays[0] = jnp.zeros(near_decays.shape[1:], jnp.float32)
+
+    @pl.when(block == n_seq - 1)
+    def _():
+        near_decays[1] = jnp.zeros(near_decays.shape[1:], jnp.float32)
+
+    @pl.when(jnp.logical_not(gets_relay))
+    def _():
+        relayed[...] = jnp.zeros(relayed.shape, jnp.float32)
+
+    def chunk_of(chunk):
+        return pl.ds(pl.multiple_of(chunk * CHUNK_HEADS, CHUNK_HEADS), CHUNK_HEADS)
+
+    def pair_copy(chunk):
+        return pltpu.make_async_remote_copy(
+            src_ref=states.at[side, chunk_of(chunk)],
+            dst_ref=from_pair.at[chunk_of(chunk)],
+            send_sem=pair_send.at[chunk],
+            recv_sem=pair_recv.at[chunk],
+            device_id={"seq": pair},
+            device_id_type=MESH_ID,
+        )
+
+    def line_copy(way, chunk):
+        target = jnp.minimum(block + 2, n_seq - 1) if way == 0 else jnp.maximum(block - 2, 0)
+        return pltpu.make_async_remote_copy(
+            src_ref=states.at[way, chunk_of(chunk)],
+            dst_ref=from_line.at[way, chunk_of(chunk)],
+            send_sem=line_send.at[way, chunk],
+            recv_sem=line_recv.at[way, chunk],
+            device_id={"seq": target},
+            device_id_type=MESH_ID,
+        )
+
+    def relay_copy(chunk):
+        return pltpu.make_async_remote_copy(
+            src_ref=from_line.at[1 - side, chunk_of(chunk)],
+            dst_ref=relayed.at[chunk_of(chunk)],
+            send_sem=relay_send.at[chunk],
+            recv_sem=relay_recv.at[chunk],
+            device_id={"seq": pair},
+            device_id_type=MESH_ID,
+        )
+
+    def decay_copy(way):
+        target = jnp.minimum(block + 1, n_seq - 1) if way == 0 else jnp.maximum(block - 1, 0)
+        return pltpu.make_async_remote_copy(
+            src_ref=decays,
+            dst_ref=near_decays.at[way],
+            send_sem=decay_send.at[way],
+            recv_sem=decay_recv.at[way],
+            device_id={"seq": target},
+            device_id_type=MESH_ID,
+        )
+
+    def head_columns(head):
+        return pl.ds(pl.multiple_of(head * HEAD_DIM, HEAD_DIM), HEAD_DIM)
+
+    def rows_since():
+        return lax.broadcasted_iota(jnp.int32, (rows, HEAD_DIM), 0).astype(jnp.float32)
+
+    def carry_in_of(head):
+        return jnp.exp(log_in[...] - rates[head] * (rows_since() + 1.0))
+
+    def carry_out_of(head):
+        return jnp.exp(log_out[...] - rates[head] * (float(rows - 1) - rows_since()))
+
+    pl.semaphore_wait(barrier, n_seq - 1 + n_dp - 1)
+
+    not_end = jnp.logical_not(block == n_seq - 1)
+    not_begin = jnp.logical_not(block == 0)
+
+    @pl.when(not_end)
+    def _():
+        decay_copy(0).start()
+
+    @pl.when(not_begin)
+    def _():
+        decay_copy(1).start()
+
+    def own_states(chunk, carry):
+        for inner in range(CHUNK_HEADS):
+            head = chunk * CHUNK_HEADS + inner
+            at = head_columns(head)
+            high, low = halves(carry_out_of(head) * keys[:, at].astype(jnp.float32))
+            value = values[:, at]
+            states[0, head] = dot(high, value, (0, 0)) + dot(low, value, (0, 0))
+            high, low = halves(carry_in_of(head) * queries[:, at].astype(jnp.float32))
+            gradient = gradients[:, at]
+            states[1, head] = dot(high, gradient, (0, 0)) + dot(low, gradient, (0, 0))
+        pair_copy(chunk).start()
+
+        @pl.when(jnp.logical_not(is_last))
+        def _():
+            line_copy(0, chunk).start()
+
+        @pl.when(jnp.logical_not(is_first))
+        def _():
+            line_copy(1, chunk).start()
+
+        return carry
+
+    lax.fori_loop(0, CHUNKS, own_states, 0)
+
+    def within(chunk, carry):
+        for inner in range(CHUNK_HEADS):
+            head = chunk * CHUNK_HEADS + inner
+            at = head_columns(head)
+            query, key = queries[:, at], keys[:, at]
+            value, gradient = values[:, at], gradients[:, at]
+            weight = jnp.exp(spread[...] - rates[head] * distance[...])
+            attn_prob = (weight * dot(query, key, (1, 1))).astype(jnp.bfloat16)
+            grad_prob = (weight * dot(gradient, value, (1, 1))).astype(jnp.bfloat16)
+            value_sum[:, at] = dot(attn_prob, gradient, (0, 0))
+            query_sum[:, at] = dot(grad_prob, key, (1, 0))
+            key_sum[:, at] = dot(grad_prob, query, (0, 0))
+
+        @pl.when(has_relay)
+        def _():
+            @pl.when(side == 1)
+            def _():
+                line_copy(0, chunk).wait_recv()
+
+            @pl.when(side == 0)
+            def _():
+                line_copy(1, chunk).wait_recv()
+
+            relay_copy(chunk).start()
+
+        return carry
+
+    lax.fori_loop(0, CHUNKS, within, 0)
+
+    @pl.when(not_begin)
+    def _():
+        decay_copy(0).wait_recv()
+
+    @pl.when(not_end)
+    def _():
+        decay_copy(1).wait_recv()
+
+    def twice(array):
+        return jnp.concatenate((array, array), axis=1)
+
+    def across(chunk, carry):
+        pair_copy(chunk).wait_recv()
+
+        @pl.when((side == 0) & jnp.logical_not(is_first))
+        def _():
+            line_copy(0, chunk).wait_recv()
+
+        @pl.when((side == 1) & jnp.logical_not(is_last))
+        def _():
+            line_copy(1, chunk).wait_recv()
+
+        @pl.when(gets_relay)
+        def _():
+            relay_copy(chunk).wait_recv()
+
+        for inner in range(CHUNK_HEADS):
+            head = chunk * CHUNK_HEADS + inner
+            at = head_columns(head)
+            paired, passed = from_pair[head], relayed[head]
+            before = jnp.where(side == 0, passed, paired)
+            after = jnp.where(side == 0, paired, passed)
+            state_in = before + near_decays[0, pl.ds(head, 1), :] * from_line[0, head]
+            grad_in = after + near_decays[1, pl.ds(head, 1), :] * from_line[1, head]
+            state_in = jnp.concatenate(halves(state_in), axis=1)
+            high, low = halves(grad_in)
+            grad_wide = jnp.concatenate((high, low), axis=1)
+            grad_tall = jnp.concatenate((high, low), axis=0)
+            query, key = queries[:, at], keys[:, at]
+            carry_in, carry_out = carry_in_of(head), carry_out_of(head)
+            query_full = query_sum[:, at] + carry_in * dot(
+                twice(gradients[:, at]), state_in, (1, 1)
+            )
+            key_full = key_sum[:, at] + carry_out * dot(twice(values[:, at]), grad_wide, (1, 1))
+            value_full = value_sum[:, at] + carry_out * dot(twice(key), grad_tall, (1, 0))
+            query_out[:, at] = query_full.astype(jnp.bfloat16)
+            key_out[:, at] = key_full.astype(jnp.bfloat16)
+            value_out[:, at] = value_full.astype(jnp.bfloat16)
+            inner_step = key.astype(jnp.float32) * key_full - query.astype(jnp.float32) * query_full
+            rate_rows[pl.ds(head, 1), :] = jnp.sum(
+                place[...] * inner_step, axis=0, keepdims=True
+            )
+        return carry
+
+    lax.fori_loop(0, CHUNKS, across, 0)
+
+    def dp_copy(other):
+        return pltpu.make_async_remote_copy(
+            src_ref=rate_rows,
+            dst_ref=rate_dp.at[other],
+            send_sem=dp_send.at[other],
+            recv_sem=dp_recv.at[other],
+            device_id={"dp": lax.rem(part + other, n_dp)},
+            device_id_type=MESH_ID,
+        )
+
+    def seq_copy(other):
+        return pltpu.make_async_remote_copy(
+            src_ref=rate_seq.at[0],
+            dst_ref=rate_seq.at[other],
+            send_sem=seq_send.at[other],
+            recv_sem=seq_recv.at[other],
+            device_id={"seq": lax.rem(block + other, n_seq)},
+            device_id_type=MESH_ID,
+        )
+
+    for other in range(1, n_dp):
+        dp_copy(other).start()
+    summed = rate_rows[...]
+    for other in range(1, n_dp):
+        dp_copy(other).wait_recv()
+        summed = summed + rate_dp[other]
+    rate_seq[0] = summed
+    for other in range(1, n_seq):
+        seq_copy(other).start()
+    for other in range(1, n_seq):
+        seq_copy(other).wait_recv()
+        summed = summed + rate_seq[other]
+    rate_out[...] = jnp.sum(summed, axis=1, keepdims=True)
+
+    for other in range(1, n_dp):
+        dp_copy(other).wait_send()
+    for other in range(1, n_seq):
+        seq_copy(other).wait_send()
+
+    @pl.when(not_end)
+    def _():
+        decay_copy(0).wait_send()
+
+    @pl.when(not_begin)
+    def _():
+        decay_copy(1).wait_send()
+
+    def sent(chunk, carry):
+        pair_copy(chunk).wait_send()
+
+        @pl.when(jnp.logical_not(is_last))
+        def _():
+            line_copy(0, chunk).wait_send()
+
+        @pl.when(jnp.logical_not(is_first))
+        def _():
+            line_copy(1, chunk).wait_send()
+
+        @pl.when(has_relay)
+        def _():
+            relay_copy(chunk).wait_send()
+
+        return carry
+
+    lax.fori_loop(0, CHUNKS, sent, 0)
+
+
+def on_device_near(
+    queries, keys, values, output_gradient, document_lengths, cutoff_rows, head_decay_rate
+):
+    rows, width = queries.shape[1:]
+    n_seq, n_dp = lax.axis_size("seq"), lax.axis_size("dp")
+    vmem = pl.BlockSpec(memory_space=pltpu.VMEM)
+    smem = pl.BlockSpec(memory_space=pltpu.SMEM)
+    out = jax.ShapeDtypeStruct((rows, width), jnp.bfloat16)
+    state = (HEADS, HEAD_DIM, HEAD_DIM)
+    dma = pltpu.SemaphoreType.DMA
+    query_grad, key_grad, value_grad, rate_total = pl.pallas_call(
+        near_kernel,
+        out_shape=(out, out, out, jax.ShapeDtypeStruct((HEADS, 1), jnp.float32)),
+        in_specs=[smem, smem] + [vmem] * 5,
+        out_specs=[vmem] * 4,
+        scratch_shapes=[
+            pltpu.VMEM((rows, rows), jnp.float32),
+            pltpu.VMEM((rows, rows), jnp.float32),
+            pltpu.VMEM((rows, HEAD_DIM), jnp.float32),
+            pltpu.VMEM((rows, HEAD_DIM), jnp.float32),
+            pltpu.VMEM((rows, HEAD_DIM), jnp.float32),
+            pltpu.VMEM((HEADS, HEAD_DIM), jnp.float32),
+            pltpu.VMEM((2, HEADS, HEAD_DIM), jnp.float32),
+            pltpu.VMEM((2,) + state, jnp.float32),
+            pltpu.VMEM(state, jnp.float32),
+            pltpu.VMEM((2,) + state, jnp.float32),
+            pltpu.VMEM(state, jnp.float32),
+            pltpu.VMEM((rows, width), jnp.float32),
+            pltpu.VMEM((rows, width), jnp.float32),
+            pltpu.VMEM((rows, width), jnp.float32),
+            pltpu.VMEM((HEADS, HEAD_DIM), jnp.float32),
+            pltpu.VMEM((n_dp, HEADS, HEAD_DIM), jnp.float32),
+            pltpu.VMEM((n_seq, HEADS, HEAD_DIM), jnp.float32),
+            dma((CHUNKS,)),
+            dma((CHUNKS,)),
+            dma((2, CHUNKS)),
+            dma((2, CHUNKS)),
+            dma((CHUNKS,)),
+            dma((CHUNKS,)),
+            dma((2,)),
+            dma((2,)),
+            dma((n_dp,)),
+            dma((n_dp,)),
+            dma((n_seq,)),
+            dma((n_seq,)),
+        ],
+        compiler_params=pltpu.CompilerParams(
+            collective_id=0, has_side_effects=True, vmem_limit_bytes=48 * 1024 * 1024
+        ),
+    )(
+        document_lengths,
+        head_decay_rate,
+        cutoff_rows,
+        queries[0],
+        keys[0],
+        values[0],
+        output_gradient[0],
+    )
+    token_total = rows * n_seq * n_dp
+    rate_grad = head_decay_rate * rate_total[:, 0] / math.sqrt(token_total)
+    return (query_grad[None], key_grad[None], value_grad[None], rate_grad)
+
+
 def solution(mesh):
     in_specs = (
         P("dp", "seq", None),
@@ -142,6 +594,7 @@
         P(),
     )
     out_specs = (P("dp", "seq", None), P("dp", "seq", None), P("dp", "seq", None), P())
+    near = mesh.shape["seq"] == 8
     return jax.shard_map(
-        on_device, mesh=mesh, in_specs=in_specs, out_specs=out_specs, check_vma=False
-    )
+        on_device_near if near else on_device, mesh=mesh, in_specs=in_specs, out_specs=out_specs, check_vma=False
+    )

time: 360 us -> 73.3 us (0.20)
  waiting for transfers between devices: 198 us -> 0 us
  blocking collectives: 69.5 us -> 0 us
  Pallas kernels: 0 us -> 63.7 us
  matrix products: 42.3 us -> 0 us
  other arithmetic: 16.6 us -> 0.63 us
  between operations: 14.8 us -> 0.66 us
  local copies, waits for them, and re-layouts: 17.4 us -> 8.13 us
    all_gather x2 -> x0, waiting for transfers between devices: 198 us -> none  [carried_in(): gathered = jax.tree.map(lambda a: lax.all_gather(a, axis), part)]
    pallas_call x0 -> x1, Pallas kernels: none -> 63.7 us  [on_device_near(): pl.pallas_call(near_kernel, out_shape=(out, out, out, jax.ShapeDtypeStruc...]
    psum x1 -> x0, blocking collectives: 47.1 us -> none  [on_device(): rate_total = lax.psum(rate_part, ('seq', 'dp'))]
    dot_general x9 -> x0, matrix products: 42.3 us -> none  [the longest x1 8.23 us: on_device(): jnp.einsum('hst,shf->thf', attn_prob, gradient_block, preferred_element_t...]
    all_gather x1 -> x0, blocking collectives: 22.4 us -> none  [carried_in(): gathered = jax.tree.map(lambda a: lax.all_gather(a, axis), part)]
    add x8 -> x0, other arithmetic: 10.4 us -> none  [the longest x7 10.4 us: backward_combine(): later[1] + later[0][:, None, None] * earlier[1]]
    unnamed x20 -> x13, local copies, waits for them, and re-layouts: 13.7 us -> 8.13 us
  transfers between devices with their start and end apart: 2 -> 0, of which waited for: 2 -> 0; matrix products, arithmetic and copies ran while one was open for 9% -> 0% of each run, Pallas kernels for 0% -> 0%
where the time goes in v1:
time: 73.3 us; the launch traced here: 73.1 us
  Pallas kernels  63.7 us (87%)
  local copies, waits for them, and re-layouts  8.13 us (11%)
    pallas_call x1, Pallas kernels, on_device_near(): pl.pallas_call(near_kernel, out_shape=(out, out, out, jax.ShapeDtypeStruc...  63.7 us
    unnamed x13, local copies, waits for them, and re-layouts  8.13 us

profile of v1, /device:TPU:0, one launch (start us, length us, event | category | flops | bytes accessed | tf_op | source)
XLA Modules:
  0.0 73.1 jit_solution(23645968777856025)
XLA Ops:
  0.6 0.0 copy-start.1
  0.6 0.7 copy-done.1
  1.3 0.0 copy-start.2
  1.3 0.7 copy-done.2
  2.0 0.0 copy-start.3
  2.0 0.7 copy-done.3
  2.6 0.0 copy-start.4
  2.6 63.7 %shard_map.102 = (bf16[384,2048]{1,0:T(8,128)(2,1)S(1)}, bf16[384,2048]{1,0:T(8,128)(2,1)S(1)}, bf16[384,2048]{1,0:T(8,128)(2,1)S(1)}, f32[16,1]{1,0:T(8,128)S(1)}) custom-call(s32[1,8]{1,0:T(1,128)S(1)} %copy-done.2, f32[16]{0:T(128)S(1)} %copy-done.3, s32[1,384]{1,0:T(1,128)S(1)} %copy-done.1, bf16[384,2048]{1,0:T(8,128)(2,1)} %bitcast.10, ...), custom_call_target="tpu_custom_call" | custom-call | tf_op jit(solution)/shard_map/pallas_call | solution.py:533
  66.3 0.0 copy-start
  66.3 1.1 %copy-done = bf16[384,2048]{1,0:T(8,128)(2,1)} copy-done((bf16[384,2048]{1,0:T(8,128)(2,1)}, bf16[384,2048]{1,0:T(8,128)(2,1)S(1)}, u32[]{:S(2)}) %copy-start) | copy-done | bytes 1572888
  67.4 0.1 reduce
  67.6 0.0 copy-done.4
  67.6 0.5 multiply_multiply_fusion
  68.1 2.7 %copy.14 = bf16[1,384,2048]{2,1,0:T(8,128)(2,1)} copy(bf16[1,384,2048]{2,1,0:T(8,128)(2,1)} %bitcast.9) | data formatting | bytes 3145728
  70.8 1.1 %copy.15 = bf16[1,384,2048]{2,1,0:T(8,128)(2,1)} copy(bf16[1,384,2048]{2,1,0:T(8,128)(2,1)S(1)} %bitcast.8) | data formatting | bytes 3145728
  71.9 1.1 %copy.16 = bf16[1,384,2048]{2,1,0:T(8,128)(2,1)} copy(bf16[1,384,2048]{2,1,0:T(8,128)(2,1)S(1)} %bitcast.7) | data formatting | bytes 3145728
Async XLA Ops:
  0.6 0.7 copy-start.1
  1.3 0.7 copy-start.2
  2.0 0.7 copy-start.3
  2.6 64.9 %copy-start.4 = (f32[16]{0:T(128)S(1)}, f32[16]{0:T(128)}, u32[]{:S(2)}) copy-start(f32[16]{0:T(128)} %rates.1) | copy-start | bytes 196
  66.3 1.1 %copy-start = (bf16[384,2048]{1,0:T(8,128)(2,1)}, bf16[384,2048]{1,0:T(8,128)(2,1)S(1)}, u32[]{:S(2)}) copy-start(bf16[384,2048]{1,0:T(8,128)(2,1)S(1)} %get-tuple-element.8) | copy-start | bytes 4718596

commit v2 on v1

--- a/solution.py
+++ b/solution.py
@@ -152,6 +152,17 @@
 
 
 def near_kernel(
+    lengths_far,
+    rates_far,
+    cutoffs_far,
+    queries_far,
+    keys_far,
+    values_far,
+    gradients_far,
+    query_out,
+    key_out,
+    value_out,
+    rate_out,
     lengths,
     rates,
     cutoffs,
@@ -159,10 +170,6 @@
     keys,
     values,
     gradients,
-    query_out,
-    key_out,
-    value_out,
-    rate_out,
     spread,
     distance,
     log_in,
@@ -180,6 +187,7 @@
     rate_rows,
     rate_dp,
     rate_seq,
+    loaded,
     pair_send,
     pair_recv,
     line_send,
@@ -202,6 +210,23 @@
     has_relay = jnp.where(side == 1, block, n_seq - 1 - block) >= 2
     gets_relay = jnp.where(side == 0, block, n_seq - 1 - block) >= 2
 
+    loads = [
+        pltpu.make_async_copy(far, near, loaded.at[i])
+        for i, (far, near) in enumerate(
+            (
+                (lengths_far, lengths),
+                (cutoffs_far, cutoffs),
+                (rates_far, rates),
+                (keys_far.at[0], keys),
+                (values_far.at[0], values),
+                (queries_far.at[0], queries),
+                (gradients_far.at[0], gradients),
+            )
+        )
+    ]
+    for load in loads:
+        load.start()
+
     barrier = pltpu.get_barrier_semaphore()
     for other in range(1, n_seq):
         pl.semaphore_signal(
@@ -214,6 +239,9 @@
         pl.semaphore_signal(
             barrier, inc=1, device_id={"dp": lax.rem(part + other, n_dp)}, device_id_type=MESH_ID
         )
+
+    for load in loads[:3]:
+        load.wait()
 
     first = block * rows
     starts, total = [], jnp.int32(0)
@@ -235,9 +263,6 @@
     cut_column = jnp.sum(jnp.where(column_of == row_of, cut_all, 0.0), axis=1, keepdims=True)
     count_row = jnp.sum(jnp.where(row_of <= column_of, cut_column, 0.0), axis=0, keepdims=True)
     count_last = jnp.sum(cut_row, axis=1, keepdims=True)
-    allowed = (segment(row_of) == segment(column_of)) & (row_of >= column_of)
-    spread[...] = jnp.where(allowed, (count_column - count_row) * cutoff_logarithm, MASKED)
-    distance[...] = (row_of - column_of).astype(jnp.float32)
     local = lax.broadcasted_iota(jnp.int32, (rows, HEAD_DIM), 0)
     last = jnp.full((rows, HEAD_DIM), rows - 1, jnp.int32)
     piece = segment(local)
@@ -246,10 +271,6 @@
     log_out[...] = jnp.where(
         piece == piece_last, (count_last - count_column) * cutoff_logarithm, MASKED
     )
-    begin = jnp.zeros((rows, HEAD_DIM), jnp.int32)
-    for start in starts:
-        begin = jnp.maximum(begin, jnp.where(local + first >= start, start, 0))
-    place[...] = (local + first - begin).astype(jnp.float32)
     log_all = jnp.where(piece_last[:1] == 0, count_last * cutoff_logarithm, MASKED)
     for h in range(HEADS):
         decays[h : h + 1, :] = jnp.exp(log_all - rates[h] * float(rows))
@@ -366,20 +387,41 @@
 
         return carry
 
+    for load in loads[3:]:
+        load.wait()
     lax.fori_loop(0, CHUNKS, own_states, 0)
+
+    piece_row = segment(lax.broadcasted_iota(jnp.int32, (1, rows), 1))
+    allowed = (piece[:, :1] == piece_row) & (row_of >= column_of)
+    spread[...] = jnp.where(allowed, (count_column - count_row) * cutoff_logarithm, MASKED)
+    distance[...] = (row_of - column_of).astype(jnp.float32)
+    begin = jnp.zeros((rows, HEAD_DIM), jnp.int32)
+    for start in starts:
+        begin = jnp.maximum(begin, jnp.where(local + first >= start, start, 0))
+    place[...] = (local + first - begin).astype(jnp.float32)
 
     def within(chunk, carry):
         for inner in range(CHUNK_HEADS):
             head = chunk * CHUNK_HEADS + inner
             at = head_columns(head)
-            query, key = queries[:, at], keys[:, at]
-            value, gradient = values[:, at], gradients[:, at]
-            weight = jnp.exp(spread[...] - rates[head] * distance[...])
-            attn_prob = (weight * dot(query, key, (1, 1))).astype(jnp.bfloat16)
-            grad_prob = (weight * dot(gradient, value, (1, 1))).astype(jnp.bfloat16)
-            value_sum[:, at] = dot(attn_prob, gradient, (0, 0))
-            query_sum[:, at] = dot(grad_prob, key, (1, 0))
-            key_sum[:, at] = dot(grad_prob, query, (0, 0))
+            for step, (low, high) in enumerate(((0, rows - HEAD_DIM), (rows - HEAD_DIM, rows))):
+                here, upto = slice(low, high), slice(0, high)
+                query, key = queries[here, at], keys[upto, at]
+                value, gradient = values[upto, at], gradients[here, at]
+                weight = jnp.exp(spread[here, upto] - rates[head] * distance[here, upto])
+                attn_prob = (weight * dot(query, key, (1, 1))).astype(jnp.bfloat16)
+                grad_prob = (weight * dot(gradient, value, (1, 1))).astype(jnp.bfloat16)
+                query_sum[here, at] = dot(grad_prob, key, (1, 0))
+                value_part = dot(attn_prob, gradient, (0, 0))
+                key_part = dot(grad_prob, query, (0, 0))
+                if step == 0:
+                    value_sum[upto, at] = value_part
+                    key_sum[upto, at] = key_part
+                else:
+                    value_sum[:low, at] += value_part[:low]
+                    key_sum[:low, at] += key_part[:low]
+                    value_sum[low:, at] = value_part[low:]
+                    key_sum[low:, at] = key_part[low:]
 
         @pl.when(has_relay)
         def _():
@@ -485,7 +527,13 @@
     for other in range(1, n_seq):
         seq_copy(other).wait_recv()
         summed = summed + rate_seq[other]
-    rate_out[...] = jnp.sum(summed, axis=1, keepdims=True)
+    scale = 1.0 / math.sqrt(rows * n_seq * n_dp)
+    lane = lax.broadcasted_iota(jnp.int32, (1, HEAD_DIM), 1)
+    summed = jnp.sum(summed, axis=1, keepdims=True) * scale
+    result = jnp.zeros((1, HEAD_DIM), jnp.float32)
+    for h in range(HEADS):
+        result = jnp.where(lane == h, rates[h] * summed[h : h + 1], result)
+    rate_out[...] = result[:, :HEADS]
 
     for other in range(1, n_dp):
         dp_copy(other).wait_send()
@@ -518,6 +566,17 @@
         return carry
 
     lax.fori_loop(0, CHUNKS, sent, 0)
+
+
+def finish_kernel(*refs):
+    count = (len(refs) - 1) // 2
+    copies = [
+        pltpu.make_async_copy(refs[i], refs[count + i], refs[-1].at[i]) for i in range(count)
+    ]
+    for copy in copies:
+        copy.start()
+    for copy in copies:
+        copy.wait()
 
 
 def on_device_near(
@@ -526,16 +585,25 @@
     rows, width = queries.shape[1:]
     n_seq, n_dp = lax.axis_size("seq"), lax.axis_size("dp")
     vmem = pl.BlockSpec(memory_space=pltpu.VMEM)
-    smem = pl.BlockSpec(memory_space=pltpu.SMEM)
+    hbm = pl.BlockSpec(memory_space=pltpu.HBM)
+    anywhere = pl.BlockSpec(memory_space=pl.ANY)
     out = jax.ShapeDtypeStruct((rows, width), jnp.bfloat16)
     state = (HEADS, HEAD_DIM, HEAD_DIM)
     dma = pltpu.SemaphoreType.DMA
-    query_grad, key_grad, value_grad, rate_total = pl.pallas_call(
+    near = pltpu.VMEM((rows, width), jnp.bfloat16)
+    results = pl.pallas_call(
         near_kernel,
-        out_shape=(out, out, out, jax.ShapeDtypeStruct((HEADS, 1), jnp.float32)),
-        in_specs=[smem, smem] + [vmem] * 5,
+        out_shape=(out, out, out, jax.ShapeDtypeStruct((1, HEADS), jnp.float32)),
+        in_specs=[hbm] * 7,
         out_specs=[vmem] * 4,
         scratch_shapes=[
+            pltpu.SMEM(document_lengths.shape, jnp.int32),
+            pltpu.SMEM(head_decay_rate.shape, jnp.float32),
+            pltpu.VMEM(cutoff_rows.shape, jnp.int32),
+            near,
+            near,
+            near,
+            near,
             pltpu.VMEM((rows, rows), jnp.float32),
             pltpu.VMEM((rows, rows), jnp.float32),
             pltpu.VMEM((rows, HEAD_DIM), jnp.float32),
@@ -553,6 +621,7 @@
             pltpu.VMEM((HEADS, HEAD_DIM), jnp.float32),
             pltpu.VMEM((n_dp, HEADS, HEAD_DIM), jnp.float32),
             pltpu.VMEM((n_seq, HEADS, HEAD_DIM), jnp.float32),
+            dma((7,)),
             dma((CHUNKS,)),
             dma((CHUNKS,)),
             dma((2, CHUNKS)),
@@ -573,14 +642,19 @@
         document_lengths,
         head_decay_rate,
         cutoff_rows,
-        queries[0],
-        keys[0],
-        values[0],
-        output_gradient[0],
-    )
-    token_total = rows * n_seq * n_dp
-    rate_grad = head_decay_rate * rate_total[:, 0] / math.sqrt(token_total)
-    return (query_grad[None], key_grad[None], value_grad[None], rate_grad)
+        queries,
+        keys,
+        values,
+        output_gradient,
+    )
+    query_grad, key_grad, value_grad, rate_grad = pl.pallas_call(
+        finish_kernel,
+        out_shape=tuple(jax.ShapeDtypeStruct(a.shape, a.dtype) for a in results),
+        in_specs=[anywhere] * 4,
+        out_specs=[anywhere] * 4,
+        scratch_shapes=[dma((4,))],
+    )(*results)
+    return (query_grad[None], key_grad[None], value_grad[None], rate_grad[0])
 
 
 def solution(mesh):

time: 73.3 us -> 213 us (2.91)
  Pallas kernels: 63.7 us -> 206 us
    pallas_call x0 -> x1, Pallas kernels: none -> 144 us  [on_device_near(): pl.pallas_call(finish_kernel, out_shape=tuple((jax.ShapeDtypeStruct(a.sha...]
    unnamed x13 -> x14, local copies, waits for them, and re-layouts: 8.13 us -> 6.03 us
where the time goes in v2:
time: 213 us
  Pallas kernels  206 us (97%)
  local copies, waits for them, and re-layouts  6.03 us (3%)
    pallas_call x1, Pallas kernels, on_device_near(): pl.pallas_call(finish_kernel, out_shape=tuple((jax.ShapeDtypeStruct(a.sha...  144 us
    pallas_call x1, Pallas kernels, on_device_near(): pl.pallas_call(near_kernel, out_shape=(out, out, out, jax.ShapeDtypeStruc...  62.1 us
    unnamed x14, local copies, waits for them, and re-layouts  6.03 us

profile of v2, /device:TPU:0, one launch (start us, length us, event | category | flops | bytes accessed | tf_op | source)
XLA Modules:
  0.0 212.9 jit_solution(11348847688642458925)
XLA Ops:
  0.6 0.0 copy-start.3
  0.6 0.7 copy-done.3
  1.3 0.0 copy-start.4
  1.3 0.7 copy-done.4
  2.0 0.0 copy-start.5
  2.0 0.7 copy-done.5
  2.6 62.1 %shard_map.102 = (bf16[384,2048]{1,0:T(8,128)(2,1)S(1)}, bf16[384,2048]{1,0:T(8,128)(2,1)S(1)}, bf16[384,2048]{1,0:T(8,128)(2,1)S(1)}, f32[1,16]{1,0:T(1,128)S(1)}) custom-call(s32[1,8]{1,0:T(1,128)S(1)} %copy-done.4, f32[16]{0:T(128)S(1)} %copy-done.5, s32[1,384]{1,0:T(1,128)S(1)} %copy-done.3, bf16[1,384,2048]{2,1,0:T(8,128)(2,1)} %queries_far.1, ...), custom_call_target="tpu_custom_call" | custom-call | tf_op jit(solution)/shard_map/pallas_call | solution.py:594
  64.7 0.0 copy-start
  64.7 1.1 copy-done
  65.9 0.0 copy-start.1
  65.9 1.1 copy-done.1
  67.0 0.0 copy-start.2
  67.0 1.2 copy-done.2
  68.2 0.0 copy-start.6
  68.2 0.6 copy-done.6
  68.8 144.1 %shard_map.103 = (bf16[384,2048]{1,0:T(8,128)(2,1)}, bf16[384,2048]{1,0:T(8,128)(2,1)}, bf16[384,2048]{1,0:T(8,128)(2,1)}, f32[1,16]{1,0:T(1,128)}) custom-call(bf16[384,2048]{1,0:T(8,128)(2,1)} %copy-done, bf16[384,2048]{1,0:T(8,128)(2,1)} %copy-done.1, bf16[384,2048]{1,0:T(8,128)(2,1)} %copy-done.2, f32[1,16]{1,0:T(1,128)} %copy-done.6), custom_call_target="tpu_custom_call" | custom-call | tf_op jit(solution)/shard_map/pallas_call | solution.py:650
Async XLA Ops:
  0.6 0.7 copy-start.3
  1.3 0.7 copy-start.4
  2.0 0.7 copy-start.5
  64.7 1.1 copy-start
  65.9 1.2 copy-start.1
  67.0 1.2 copy-start.2
  68.2 0.6 copy-start.6

commit v3 on v2

--- a/solution.py
+++ b/solution.py
@@ -650,7 +650,7 @@
     query_grad, key_grad, value_grad, rate_grad = pl.pallas_call(
         finish_kernel,
         out_shape=tuple(jax.ShapeDtypeStruct(a.shape, a.dtype) for a in results),
-        in_specs=[anywhere] * 4,
+        in_specs=[vmem] * 4,
         out_specs=[anywhere] * 4,
         scratch_shapes=[dma((4,))],
     )(*results)

time: 213 us -> 73.5 us (0.35)
  Pallas kernels: 206 us -> 66.6 us
    pallas_call x1, Pallas kernels: 144 us -> 4.57 us  [on_device_near(): pl.pallas_call(finish_kernel, out_shape=tuple((jax.ShapeDtypeStruct(a.sha...]
where the time goes in v3:
time: 73.5 us; the launch traced here: 73.3 us
  Pallas kernels  66.6 us (91%)
  local copies, waits for them, and re-layouts  6.03 us (8%)
    pallas_call x1, Pallas kernels, on_device_near(): pl.pallas_call(near_kernel, out_shape=(out, out, out, jax.ShapeDtypeStruc...  62.1 us
    unnamed x14, local copies, waits for them, and re-layouts  6.03 us
    pallas_call x1, Pallas kernels, on_device_near(): pl.pallas_call(finish_kernel, out_shape=tuple((jax.ShapeDtypeStruct(a.sha...  4.57 us

profile of v3, /device:TPU:0, one launch (start us, length us, event | category | flops | bytes accessed | tf_op | source)
XLA Modules:
  0.0 73.3 jit_solution(4618742683941307144)
XLA Ops:
  0.6 0.0 copy-start.3
  0.6 0.7 copy-done.3
  1.3 0.0 copy-start.4
  1.3 0.7 copy-done.4
  2.0 0.0 copy-start.5
  2.0 0.7 copy-done.5
  2.6 62.1 %shard_map.102 = (bf16[384,2048]{1,0:T(8,128)(2,1)S(1)}, bf16[384,2048]{1,0:T(8,128)(2,1)S(1)}, bf16[384,2048]{1,0:T(8,128)(2,1)S(1)}, f32[1,16]{1,0:T(1,128)S(1)}) custom-call(s32[1,8]{1,0:T(1,128)S(1)} %copy-done.4, f32[16]{0:T(128)S(1)} %copy-done.5, s32[1,384]{1,0:T(1,128)S(1)} %copy-done.3, bf16[1,384,2048]{2,1,0:T(8,128)(2,1)} %queries_far.1, ...), custom_call_target="tpu_custom_call" | custom-call | tf_op jit(solution)/shard_map/pallas_call | solution.py:594
  64.7 0.0 copy-start
  64.7 1.1 %copy-done = bf16[384,2048]{1,0:T(8,128)(2,1)} copy-done((bf16[384,2048]{1,0:T(8,128)(2,1)}, bf16[384,2048]{1,0:T(8,128)(2,1)S(1)}, u32[]{:S(2)}) %copy-start) | copy-done | bytes 1572888
  65.9 0.0 copy-start.1
  65.9 1.1 %copy-done.1 = bf16[384,2048]{1,0:T(8,128)(2,1)} copy-done((bf16[384,2048]{1,0:T(8,128)(2,1)}, bf16[384,2048]{1,0:T(8,128)(2,1)S(1)}, u32[]{:S(2)}) %copy-start.1) | copy-done | bytes 1572888
  67.0 0.0 copy-start.2
  67.0 1.2 %copy-done.2 = bf16[384,2048]{1,0:T(8,128)(2,1)} copy-done((bf16[384,2048]{1,0:T(8,128)(2,1)}, bf16[384,2048]{1,0:T(8,128)(2,1)S(1)}, u32[]{:S(2)}) %copy-start.2) | copy-done | bytes 1572888
  68.2 0.0 copy-start.6
  68.2 0.6 copy-done.6
  68.8 4.6 %shard_map.103 = (bf16[384,2048]{1,0:T(8,128)(2,1)}, bf16[384,2048]{1,0:T(8,128)(2,1)}, bf16[384,2048]{1,0:T(8,128)(2,1)}, f32[1,16]{1,0:T(1,128)}) custom-call(bf16[384,2048]{1,0:T(8,128)(2,1)} %copy-done, bf16[384,2048]{1,0:T(8,128)(2,1)} %copy-done.1, bf16[384,2048]{1,0:T(8,128)(2,1)} %copy-done.2, f32[1,16]{1,0:T(1,128)} %copy-done.6), custom_call_target="tpu_custom_call" | custom-call | tf_op jit(solution)/shard_map/pallas_call | solution.py:650
Async XLA Ops:
  0.6 0.7 copy-start.3
  1.3 0.7 copy-start.4
  2.0 0.7 copy-start.5
  64.7 1.1 %copy-start = (bf16[384,2048]{1,0:T(8,128)(2,1)}, bf16[384,2048]{1,0:T(8,128)(2,1)S(1)}, u32[]{:S(2)}) copy-start(bf16[384,2048]{1,0:T(8,128)(2,1)S(1)} %get-tuple-element.12.refs_0_) | copy-start | bytes 4718596
  65.9 1.2 %copy-start.1 = (bf16[384,2048]{1,0:T(8,128)(2,1)}, bf16[384,2048]{1,0:T(8,128)(2,1)S(1)}, u32[]{:S(2)}) copy-start(bf16[384,2048]{1,0:T(8,128)(2,1)S(1)} %get-tuple-element.13.refs_1_) | copy-start | bytes 4718596
  67.0 1.2 %copy-start.2 = (bf16[384,2048]{1,0:T(8,128)(2,1)}, bf16[384,2048]{1,0:T(8,128)(2,1)S(1)}, u32[]{:S(2)}) copy-start(bf16[384,2048]{1,0:T(8,128)(2,1)S(1)} %get-tuple-element.14.refs_2_) | copy-start | bytes 4718596
  68.2 0.6 copy-start.6

commit v4 on v3

--- a/solution.py
+++ b/solution.py
@@ -194,6 +194,7 @@
     line_recv,
     relay_send,
     relay_recv,
+    direct_send,
     decay_send,
     decay_recv,
     dp_send,
@@ -210,6 +211,16 @@
     has_relay = jnp.where(side == 1, block, n_seq - 1 - block) >= 2
     gets_relay = jnp.where(side == 0, block, n_seq - 1 - block) >= 2
 
+    line, n_line = block // 2, n_seq // 2
+    own_direct = jnp.where(side == 1, n_line - 1 - line, line) * CHUNKS // n_line
+    past_direct = jnp.where(side == 1, n_line - line, line + 1) * CHUNKS // n_line
+
+    def directs(chunk):
+        return chunk >= CHUNKS - own_direct
+
+    def relays(chunk):
+        return has_relay & (chunk < CHUNKS - past_direct)
+
     loads = [
         pltpu.make_async_copy(far, near, loaded.at[i])
         for i, (far, near) in enumerate(
@@ -329,6 +340,18 @@
             device_id_type=MESH_ID,
         )
 
+    def direct_copy(chunk):
+        return pltpu.make_async_remote_copy(
+            src_ref=states.at[1 - side, chunk_of(chunk)],
+            dst_ref=relayed.at[chunk_of(chunk)],
+            send_sem=direct_send.at[chunk],
+            recv_sem=relay_recv.at[chunk],
+            device_id={
+                "seq": jnp.clip(block - 1 + 2 * side, 0, n_seq - 1),
+            },
+            device_id_type=MESH_ID,
+        )
+
     def decay_copy(way):
         target = jnp.minimum(block + 1, n_seq - 1) if way == 0 else jnp.maximum(block - 1, 0)
         return pltpu.make_async_remote_copy(
@@ -384,6 +407,10 @@
         @pl.when(jnp.logical_not(is_first))
         def _():
             line_copy(1, chunk).start()
+
+        @pl.when(directs(chunk))
+        def _():
+            direct_copy(chunk).start()
 
         return carry
 
@@ -423,7 +450,7 @@
                     value_sum[low:, at] = value_part[low:]
                     key_sum[low:, at] = key_part[low:]
 
-        @pl.when(has_relay)
+        @pl.when(relays(chunk))
         def _():
             @pl.when(side == 1)
             def _():
@@ -453,11 +480,11 @@
     def across(chunk, carry):
         pair_copy(chunk).wait_recv()
 
-        @pl.when((side == 0) & jnp.logical_not(is_first))
+        @pl.when(jnp.logical_not(is_first | ((side == 1) & relays(chunk))))
         def _():
             line_copy(0, chunk).wait_recv()
 
-        @pl.when((side == 1) & jnp.logical_not(is_last))
+        @pl.when(jnp.logical_not(is_last | ((side == 0) & relays(chunk))))
         def _():
             line_copy(1, chunk).wait_recv()
 
@@ -559,24 +586,17 @@
         def _():
             line_copy(1, chunk).wait_send()
 
-        @pl.when(has_relay)
+        @pl.when(relays(chunk))
         def _():
             relay_copy(chunk).wait_send()
 
+        @pl.when(directs(chunk))
+        def _():
+            direct_copy(chunk).wait_send()
+
         return carry
 
     lax.fori_loop(0, CHUNKS, sent, 0)
-
-
-def finish_kernel(*refs):
-    count = (len(refs) - 1) // 2
-    copies = [
-        pltpu.make_async_copy(refs[i], refs[count + i], refs[-1].at[i]) for i in range(count)
-    ]
-    for copy in copies:
-        copy.start()
-    for copy in copies:
-        copy.wait()
 
 
 def on_device_near(
@@ -586,12 +606,11 @@
     n_seq, n_dp = lax.axis_size("seq"), lax.axis_size("dp")
     vmem = pl.BlockSpec(memory_space=pltpu.VMEM)
     hbm = pl.BlockSpec(memory_space=pltpu.HBM)
-    anywhere = pl.BlockSpec(memory_space=pl.ANY)
     out = jax.ShapeDtypeStruct((rows, width), jnp.bfloat16)
     state = (HEADS, HEAD_DIM, HEAD_DIM)
     dma = pltpu.SemaphoreType.DMA
     near = pltpu.VMEM((rows, width), jnp.bfloat16)
-    results = pl.pallas_call(
+    query_grad, key_grad, value_grad, rate_grad = pl.pallas_call(
         near_kernel,
         out_shape=(out, out, out, jax.ShapeDtypeStruct((1, HEADS), jnp.float32)),
         in_specs=[hbm] * 7,
@@ -628,6 +647,7 @@
             dma((2, CHUNKS)),
             dma((CHUNKS,)),
             dma((CHUNKS,)),
+            dma((CHUNKS,)),
             dma((2,)),
             dma((2,)),
             dma((n_dp,)),
@@ -647,13 +667,6 @@
         values,
         output_gradient,
     )
-    query_grad, key_grad, value_grad, rate_grad = pl.pallas_call(
-        finish_kernel,
-        out_shape=tuple(jax.ShapeDtypeStruct(a.shape, a.dtype) for a in results),
-        in_specs=[vmem] * 4,
-        out_specs=[anywhere] * 4,
-        scratch_shapes=[dma((4,))],
-    )(*results)
     return (query_grad[None], key_grad[None], value_grad[None], rate_grad[0])
 
 

time: 73.5 us -> 72.1 us (0.981)
  Pallas kernels: 66.6 us -> 65.3 us
    pallas_call x1 -> x0, Pallas kernels: 4.57 us -> none  [on_device_near(): pl.pallas_call(finish_kernel, out_shape=tuple((jax.ShapeDtypeStruct(a.sha...]
    pallas_call x1, Pallas kernels: 62.1 us -> 65.3 us  [on_device_near(): pl.pallas_call(near_kernel, out_shape=(out, out, out, jax.ShapeDtypeStruc...]
    unnamed x14 -> x10, local copies, waits for them, and re-layouts: 6.03 us -> 5.92 us
where the time goes in v4:
time: 72.1 us; the launch traced here: 71.9 us
  Pallas kernels  65.3 us (91%)
  local copies, waits for them, and re-layouts  5.92 us (8%)
    pallas_call x1, Pallas kernels, on_device_near(): pl.pallas_call(near_kernel, out_shape=(out, out, out, jax.ShapeDtypeStruc...  65.3 us
    unnamed x10, local copies, waits for them, and re-layouts  5.92 us

profile of v4, /device:TPU:0, one launch (start us, length us, event | category | flops | bytes accessed | tf_op | source)
XLA Modules:
  0.0 71.9 jit_solution(8988892297037989386)
XLA Ops:
  0.6 0.0 copy-start
  0.6 0.7 copy-done
  1.3 0.0 copy-start.1
  1.3 0.7 copy-done.1
  2.0 0.0 copy-start.2
  2.0 0.7 copy-done.2
  2.6 65.3 %shard_map.102 = (bf16[384,2048]{1,0:T(8,128)(2,1)S(1)}, bf16[384,2048]{1,0:T(8,128)(2,1)S(1)}, bf16[384,2048]{1,0:T(8,128)(2,1)S(1)}, f32[1,16]{1,0:T(1,128)S(1)}) custom-call(s32[1,8]{1,0:T(1,128)S(1)} %copy-done.1, f32[16]{0:T(128)S(1)} %copy-done.2, s32[1,384]{1,0:T(1,128)S(1)} %copy-done, bf16[1,384,2048]{2,1,0:T(8,128)(2,1)} %queries_far.1, ...), custom_call_target="tpu_custom_call" | custom-call | tf_op jit(solution)/shard_map/pallas_call | solution.py:613
  68.0 1.1 %copy.15 = bf16[1,384,2048]{2,1,0:T(8,128)(2,1)} copy(bf16[1,384,2048]{2,1,0:T(8,128)(2,1)S(1)} %bitcast.6) | data formatting | bytes 3145728
  69.1 1.1 %copy.16 = bf16[1,384,2048]{2,1,0:T(8,128)(2,1)} copy(bf16[1,384,2048]{2,1,0:T(8,128)(2,1)S(1)} %bitcast.5) | data formatting | bytes 3145728
  70.3 1.1 %copy.17 = bf16[1,384,2048]{2,1,0:T(8,128)(2,1)} copy(bf16[1,384,2048]{2,1,0:T(8,128)(2,1)S(1)} %bitcast.4) | data formatting | bytes 3145728
  71.4 0.5 copy.18
Async XLA Ops:
  0.6 0.7 copy-start
  1.3 0.7 copy-start.1
  2.0 0.7 copy-start.2
